TPU v7x, 128 devices: a whole 4x4x4 slice. The times are simulated.
128 devices in a mesh: row: 16 (over x_lo, y, core), col: 8 (over z, x_hi).
Axes of the slice: x: 4 (x_hi: 2, x_lo: 2; x = x_hi * 2 + x_lo), y: 4, z: 4, core: 2. Of those that a mesh axis runs over, the one named last changes fastest.
Arguments:
- ortho_in: bfloat16 [7168, 9216], P(('row', 'col')), may hold values from -6 to 6
Outputs:
- next_iterate: bfloat16 [7168, 9216], P(('row', 'col'))
All inputs are finite; a program needn't handle non-finite values.
Results may differ from a plain program's by a relative error of at most 0.024.
Values may be sent and summed in bfloat16 or wider, within the bound.
A program may use at most 128 MiB of HBM per device.

v0:
```python
import math
import jax
import jax.numpy as jnp
from jax import lax
from jax.sharding import PartitionSpec as P

coef_a = 3.4445
coef_b = -4.775
coef_c = 2.0315


def per_device(ortho_in):
    tile = lax.all_to_all(ortho_in, "col", split_axis=1, concat_axis=0, tiled=True)
    tile_rows = tile.shape[0]
    tile_cols = tile.shape[1]
    full_rows = tile_rows * lax.axis_size("row")
    full_cols = tile_cols * lax.axis_size("col")
    inv_square = 1.0 / (math.sqrt(full_rows) + math.sqrt(full_cols)) ** 2
    panel = lax.all_gather(tile, "row", axis=0, tiled=True)
    partial_gram = lax.dot_general(
        tile, panel, (((1,), (1,)), ((), ())), preferred_element_type=jnp.float32
    )
    gram_total = lax.psum(partial_gram.astype(jnp.bfloat16), "col").astype(jnp.float32)
    gram = (gram_total * inv_square).astype(jnp.bfloat16)
    first_f = jnp.dot(gram, panel, preferred_element_type=jnp.float32)
    first_prod = first_f.astype(jnp.bfloat16)
    second_prod = jnp.dot(
        gram,
        lax.all_gather(first_prod, "row", axis=0, tiled=True),
        preferred_element_type=jnp.float32,
    )
    iterate = (
        coef_a * tile.astype(jnp.float32)
        + coef_b * first_prod.astype(jnp.float32)
        + coef_c * second_prod
    )
    result_tile = iterate.astype(jnp.bfloat16)
    return lax.all_to_all(result_tile, "col", split_axis=0, concat_axis=1, tiled=True)


def solution(mesh):
    in_specs = (P(("row", "col"), None),)
    out_specs = P(("row", "col"), None)
    return jax.shard_map(
        per_device, mesh=mesh, in_specs=in_specs, out_specs=out_specs, check_vma=False
    )
```

profile of v0, /device:TPU:0, one launch (start us, length us, event | category | flops | bytes accessed | tf_op | source)
XLA Modules:
  0.0 553.5 jit_solution(15117017379384241305)
XLA Ops:
  6.5 0.0 all-gather.3.cloned.1.call-start
  6.5 1.3 copy.7
  7.8 24.8 %all_to_all.38 = bf16[56,8,1152]{2,0,1:T(8,128)(2,1)} all-to-all(bf16[56,8,1152]{2,0,1:T(8,128)(2,1)S(1)} %bitcast.19), channel_id=1, replica_groups=mesh['row'=16,'col'=8] {'col'}, dimensions={1} | all-to-all | bytes 2064384 | tf_op jit(solution)/shard_map/all_to_all | solution.py:13
  32.6 0.0 all-gather.3.cloned.1.call-update
  32.6 0.0 all-reduce.2.cloned.1.call-start
  32.7 87.9 %all-gather.3.cloned.1.call-done = bf16[7168,1152]{1,0:T(8,128)(2,1)} async-done(((bf16[448,1152]{1,0:T(8,128)(2,1)}), bf16[7168,1152]{1,0:T(8,128)(2,1)}) %all-gather.3.cloned.1.call-update) | async-done | bytes 16515088 | tf_op jit(solution)/shard_map/all_gather | solution.py:19
  120.6 14.0 %convolution_convert_fusion = bf16[448,7168]{1,0:T(8,128)(2,1)} fusion(bf16[448,1152]{1,0:T(8,128)(2,1)} %bitcast.16, bf16[7168,1152]{1,0:T(8,128)(2,1)} %all-gather.3.cloned.1.call-done), kind=kOutput, calls=%fused_computation.1 | convolution fusion | flops 7401963520 | bytes 23969792 | tf_op jit(solution)/shard_map/dot_general | solution.py:20
  134.6 0.0 all-reduce.2.cloned.1.call-update
  134.6 0.0 copy-start
  134.6 0.0 all-gather.5.cloned.1.call-start
  134.7 269.2 %all-reduce.2.cloned.1.call-done = bf16[448,7168]{1,0:T(8,128)(2,1)} async-done(((bf16[448,7168]{1,0:T(8,128)(2,1)}), bf16[448,7168]{1,0:T(8,128)(2,1)}) %all-reduce.2.cloned.1.call-update) | async-done | bytes 6422544 | tf_op jit(solution)/shard_map/psum | solution.py:23
  403.9 14.0 %fusion.5 = bf16[448,1152]{1,0:T(8,128)(2,1)} fusion(bf16[7168,1152]{1,0:T(8,128)(2,1)} %all-gather.3.cloned.1.call-done, bf16[448,7168]{1,0:T(8,128)(2,1)} %all-reduce.2.cloned.1.call-done), kind=kOutput, calls=%fused_computation.7 | convolution fusion | flops 7408902144 | bytes 23969792 | tf_op jit(solution)/shard_map/dot_general | solution.py:25
  417.9 0.0 all-gather.5.cloned.1.call-update
  417.9 90.2 %all-gather.5.cloned.1.call-done = bf16[7168,1152]{1,0:T(8,128)(2,1)} async-done(((bf16[448,1152]{1,0:T(8,128)(2,1)}), bf16[7168,1152]{1,0:T(8,128)(2,1)}) %all-gather.5.cloned.1.call-update) | async-done | bytes 16515088 | tf_op jit(solution)/shard_map/all_gather | solution.py:29
  508.1 0.0 copy-done
  508.1 13.7 %fusion.4 = bf16[448,1152]{1,0:T(8,128)(2,1)S(1)} fusion(bf16[7168,1152]{1,0:T(8,128)(2,1)} %all-gather.5.cloned.1.call-done, bf16[448,7168]{1,0:T(8,128)(2,1)} %all-reduce.2.cloned.1.call-done, bf16[448,1152]{1,0:T(8,128)(2,1)} %fusion.5, bf16[448,1152]{1,0:T(8,128)(2,1)S(1)} %bitcast.17), kind=kOutput, calls=%fused_computation.6 | convolution fusion | flops 7412514816 | bytes 26034176 | tf_op jit(solution)/shard_map/dot_general | solution.py:27
  521.8 24.1 %all_to_all.39 = bf16[8,56,1152]{2,1,0:T(8,128)(2,1)S(1)} all-to-all(bf16[8,56,1152]{2,1,0:T(8,128)(2,1)S(1)} %bitcast.21), channel_id=1, replica_groups=mesh['row'=16,'col'=8] {'col'}, dimensions={0} | all-to-all | bytes 2064384 | tf_op jit(solution)/shard_map/all_to_all | solution.py:38
  545.9 1.1 copy.5
Async XLA Ops:
  6.5 114.1 %all-gather.3.cloned.1.call-start = ((), (), s32[]{:S(2)}) async-start(), calls=%async_computation.2 | async-start | bytes 17547264 | tf_op jit(solution)/shard_map/all_gather | solution.py:19
  32.6 371.3 %all-reduce.2.cloned.1.call-start = ((), (), s32[]{:S(2)}) async-start(), calls=%async_computation.3 | async-start | bytes 12845056 | tf_op jit(solution)/shard_map/psum | solution.py:23
  134.6 373.5 %copy-start = (bf16[56,8,1152]{2,0,1:T(8,128)(2,1)S(1)}, bf16[56,8,1152]{2,0,1:T(8,128)(2,1)}, u32[]{:S(2)}) copy-start(bf16[56,8,1152]{2,0,1:T(8,128)(2,1)} %all_to_all.38) | copy-start | bytes 3096580
  134.6 373.5 %all-gather.5.cloned.1.call-start = ((), (), s32[]{:S(2)}) async-start(), calls=%async_computation.4 | async-start | bytes 17547264 | tf_op jit(solution)/shard_map/all_gather | solution.py:29
Sparse Core Ops, SparseCore 0:
  32.8 87.8 all-gather.2
  134.7 269.1 all-reduce.1
  418.1 90.0 all-gather.4
where the time goes:
time: 554 us
  waiting for transfers between devices  447 us (81%)
  blocking collectives  48.9 us (9%)
  matrix products  41.7 us (8%)
  between operations  13.1 us (2%)
    psum x1, waiting for transfers between devices, per_device(): lax.psum(partial_gram.astype(jnp.bfloat16), 'col').astype(jnp.float32)  269 us
    all_gather x1, waiting for transfers between devices, per_device(): lax.all_gather(first_prod, 'row', axis=0, tiled=True)  90.2 us
    all_gather x1, waiting for transfers between devices, per_device(): panel = lax.all_gather(tile, 'row', axis=0, tiled=True)  87.9 us
    all_to_all x1, blocking collectives, per_device(): lax.all_to_all(ortho_in, 'col', split_axis=1, concat_axis=0, tiled=True)  24.8 us
    all_to_all x1, blocking collectives, per_device(): lax.all_to_all(result_tile, 'col', split_axis=0, concat_axis=1, tiled=True)  24.1 us
    dot_general x1, matrix products, per_device(): first_f = jnp.dot(gram, panel, preferred_element_type=jnp.float32)  14 us
    dot_general x1, matrix products, per_device(): lax.dot_general(tile, panel, (((1,), (1,)), ((), ())), preferred_element_...  14 us
    dot_general x1, matrix products, per_device(): jnp.dot(gram, lax.all_gather(first_prod, 'row', axis=0, tiled=True), pref...  13.7 us
  transfers between devices with their start and end apart: 3, of which 3 were waited for; matrix products, arithmetic and copies ran while one was open for 0% of the time, Pallas kernels for 0%

commit v1 on v0

--- a/solution.py
+++ b/solution.py
@@ -20,7 +20,9 @@
     partial_gram = lax.dot_general(
         tile, panel, (((1,), (1,)), ((), ())), preferred_element_type=jnp.float32
     )
-    gram_total = lax.psum(partial_gram.astype(jnp.bfloat16), "col").astype(jnp.float32)
+    gram_total = jnp.sum(lax.all_gather(partial_gram.astype(jnp.bfloat16), "col"), axis=0).astype(
+        jnp.float32
+    )
     gram = (gram_total * inv_square).astype(jnp.bfloat16)
     first_f = jnp.dot(gram, panel, preferred_element_type=jnp.float32)
     first_prod = first_f.astype(jnp.bfloat16)

time: 554 us -> 802 us (1.45)
  waiting for transfers between devices: 447 us -> 672 us
  other arithmetic: 0 us -> 22.6 us
    all_gather x0 -> x1, waiting for transfers between devices: none -> 496 us  [per_device(): lax.all_gather(partial_gram.astype(jnp.bfloat16), 'col')]
    psum x1 -> x0, waiting for transfers between devices: 269 us -> none  [per_device(): lax.psum(partial_gram.astype(jnp.bfloat16), 'col').astype(jnp.float32)]
    reduce_sum x0 -> x1, other arithmetic: none -> 22.6 us  [per_device(): jnp.sum(lax.all_gather(partial_gram.astype(jnp.bfloat16), 'col'), axis=0)]
where the time goes in v1:
time: 802 us; the launch traced here: 801 us
  waiting for transfers between devices  672 us (84%)
  blocking collectives  48.9 us (6%)
  matrix products  41.8 us (5%)
  other arithmetic  22.6 us (3%)
  between operations  13.1 us (2%)
    all_gather x1, waiting for transfers between devices, per_device(): lax.all_gather(partial_gram.astype(jnp.bfloat16), 'col')  496 us
    all_gather x1, waiting for transfers between devices, per_device(): lax.all_gather(first_prod, 'row', axis=0, tiled=True)  88.3 us
    all_gather x1, waiting for transfers between devices, per_device(): panel = lax.all_gather(tile, 'row', axis=0, tiled=True)  87.9 us
    all_to_all x1, blocking collectives, per_device(): lax.all_to_all(ortho_in, 'col', split_axis=1, concat_axis=0, tiled=True)  24.8 us
    all_to_all x1, blocking collectives, per_device(): lax.all_to_all(result_tile, 'col', split_axis=0, concat_axis=1, tiled=True)  24.1 us
    reduce_sum x1, other arithmetic, per_device(): jnp.sum(lax.all_gather(partial_gram.astype(jnp.bfloat16), 'col'), axis=0)  22.6 us
  transfers between devices with their start and end apart: 3, of which 3 were waited for; matrix products, arithmetic and copies ran while one was open for 0% of the time, Pallas kernels for 0%

profile of v1, /device:TPU:0, one launch (start us, length us, event | category | flops | bytes accessed | tf_op | source)
XLA Modules:
  0.0 801.3 jit_solution(17749785359258402242)
XLA Ops:
  6.5 0.0 all-gather.5.cloned.1.call-start
  6.5 1.3 copy.7
  7.8 24.8 %all_to_all.38 = bf16[56,8,1152]{2,0,1:T(8,128)(2,1)} all-to-all(bf16[56,8,1152]{2,0,1:T(8,128)(2,1)S(1)} %bitcast.21), channel_id=1, replica_groups=mesh['row'=16,'col'=8] {'col'}, dimensions={1} | all-to-all | bytes 2064384 | tf_op jit(solution)/shard_map/all_to_all | solution.py:13
  32.6 0.0 all-gather.5.cloned.1.call-update
  32.6 0.0 all-gather.9.cloned.1.call-start
  32.7 87.9 %all-gather.5.cloned.1.call-done = bf16[7168,1152]{1,0:T(8,128)(2,1)} async-done(((bf16[448,1152]{1,0:T(8,128)(2,1)}), bf16[7168,1152]{1,0:T(8,128)(2,1)}) %all-gather.5.cloned.1.call-update) | async-done | bytes 16515088 | tf_op jit(solution)/shard_map/all_gather | solution.py:19
  120.6 14.0 %convolution_convert_fusion = bf16[448,7168]{1,0:T(8,128)(2,1)} fusion(bf16[448,1152]{1,0:T(8,128)(2,1)} %bitcast.18, bf16[7168,1152]{1,0:T(8,128)(2,1)} %all-gather.5.cloned.1.call-done), kind=kOutput, calls=%fused_computation.1 | convolution fusion | flops 7401963520 | bytes 23969792 | tf_op jit(solution)/shard_map/dot_general | solution.py:20
  134.6 0.0 all-gather.9.cloned.1.call-update
  134.6 0.2 all-gather.7.cloned.1.call-start
  134.9 496.0 %all-gather.9.cloned.1.call-done = bf16[3584,7168]{1,0:T(8,128)(2,1)} async-done(((bf16[448,7168]{1,0:T(8,128)(2,1)}), bf16[3584,7168]{1,0:T(8,128)(2,1)}) %all-gather.9.cloned.1.call-update) | async-done | bytes 51380240 | tf_op jit(solution)/shard_map/all_gather | solution.py:23
  630.9 22.6 %reduce_sum.12 = bf16[448,7168]{1,0:T(8,128)(2,1)} reduce(bf16[8,448,7168]{2,1,0:T(8,128)(2,1)} %bitcast.16, bf16[]{:T(256)} %constant.2.clone.1), dimensions={0}, to_apply=%region_0.0 | reduce | flops 22478848 | bytes 57802752 | tf_op jit(solution)/shard_map/reduce_sum | solution.py:23
  653.5 0.0 copy-start
  653.5 14.1 %fusion.5 = bf16[448,1152]{1,0:T(8,128)(2,1)} fusion(bf16[7168,1152]{1,0:T(8,128)(2,1)} %all-gather.5.cloned.1.call-done, bf16[448,7168]{1,0:T(8,128)(2,1)} %reduce_sum.12), kind=kOutput, calls=%fused_computation.7 | convolution fusion | flops 7408902144 | bytes 23969792 | tf_op jit(solution)/shard_map/dot_general | solution.py:27
  667.6 0.0 all-gather.7.cloned.1.call-update
  667.6 88.3 %all-gather.7.cloned.1.call-done = bf16[7168,1152]{1,0:T(8,128)(2,1)} async-done(((bf16[448,1152]{1,0:T(8,128)(2,1)}), bf16[7168,1152]{1,0:T(8,128)(2,1)}) %all-gather.7.cloned.1.call-update) | async-done | bytes 16515088 | tf_op jit(solution)/shard_map/all_gather | solution.py:31
  755.9 0.0 copy-done
  755.9 13.7 %fusion.4 = bf16[448,1152]{1,0:T(8,128)(2,1)S(1)} fusion(bf16[7168,1152]{1,0:T(8,128)(2,1)} %all-gather.7.cloned.1.call-done, bf16[448,7168]{1,0:T(8,128)(2,1)} %reduce_sum.12, bf16[448,1152]{1,0:T(8,128)(2,1)} %fusion.5, bf16[448,1152]{1,0:T(8,128)(2,1)S(1)} %bitcast.19), kind=kOutput, calls=%fused_computation.6 | convolution fusion | flops 7412514816 | bytes 26034176 | tf_op jit(solution)/shard_map/dot_general | solution.py:29
  769.6 24.1 %all_to_all.39 = bf16[8,56,1152]{2,1,0:T(8,128)(2,1)S(1)} all-to-all(bf16[8,56,1152]{2,1,0:T(8,128)(2,1)S(1)} %bitcast.23), channel_id=1, replica_groups=mesh['row'=16,'col'=8] {'col'}, dimensions={0} | all-to-all | bytes 2064384 | tf_op jit(solution)/shard_map/all_to_all | solution.py:40
  793.7 1.1 copy.5
Async XLA Ops:
  6.5 114.1 %all-gather.5.cloned.1.call-start = ((), (), s32[]{:S(2)}) async-start(), calls=%async_computation.2 | async-start | bytes 17547264 | tf_op jit(solution)/shard_map/all_gather | solution.py:19
  32.6 598.2 %all-gather.9.cloned.1.call-start = ((), (), s32[]{:S(2)}) async-start(), calls=%async_computation.4 | async-start | bytes 57802752 | tf_op jit(solution)/shard_map/all_gather | solution.py:23
  134.6 621.3 %all-gather.7.cloned.1.call-start = ((), (), s32[]{:S(2)}) async-start(), calls=%async_computation.3 | async-start | bytes 17547264 | tf_op jit(solution)/shard_map/all_gather | solution.py:31
  653.5 102.4 %copy-start = (bf16[56,8,1152]{2,0,1:T(8,128)(2,1)S(1)}, bf16[56,8,1152]{2,0,1:T(8,128)(2,1)}, u32[]{:S(2)}) copy-start(bf16[56,8,1152]{2,0,1:T(8,128)(2,1)} %all_to_all.38) | copy-start | bytes 3096580
Sparse Core Ops, SparseCore 0:
  32.8 87.8 all-gather.4
  134.8 496.0 all-gather.8
  667.8 88.1 all-gather.6
